TPU v7x, 128 devices: a whole 4x4x4 slice. The times are simulated.
128 devices in a mesh: item: 16 (over z, y), code: 8 (over x, core).
Axes of the slice: x: 4, y: 4, z: 4, core: 2. Of those that a mesh axis runs over, the one named last changes fastest.
Arguments:
- residuals: float32 [256, 65536], P('code', 'item'), may hold values from -6 to 6
- codebook: float32 [256, 65536], P('item', 'code'), may hold values from -6 to 6
- item_weight: float32 [65536], P('item'), may hold values from 1 to 100
- code_capacity: float32 [65536], P('code'), may hold values from 0.25 to 4
- pairs: int32 [1024, 128], P('item', 'code'), may hold values from -1 to 127, as said below
Outputs:
- item_potential: float32 [65536], P('item')
- code_potential: float32 [65536], P('code')
Inputs may be any that keep to these rules, and one draw needn't show every extreme that they name: `pairs`: each entry is -1 (no candidate) or a code block's number within the code shard of its slot column. Within one item block and one code shard the live entries are distinct, the first slot is always live, and between 1 and 8 are live; some device holds exactly 8 live slots in every item block. Every code block is named by some item block.
All inputs are finite; a program needn't handle non-finite values.
Results may differ from a plain program's by a relative error of at most 0.0003.
Values sent between devices are 32-bit elements; how exact they have to be, the bound alone decides.
A program may use at most 128 MiB of HBM per device.

v0:
```python
import math
import jax
import jax.numpy as jnp
from jax import lax
from jax.sharding import PartitionSpec as P

BLOCK = 64
ITERS = 3
masked_score = -1e30
softness_factor = 0.1


def body(residuals, codebook, item_weight, code_capacity, pairs):
    item_columns = lax.all_gather(residuals, "code", axis=0, tiled=True)
    code_cols = lax.all_gather(codebook, "item", axis=0, tiled=True)
    embedding_width = item_columns.shape[0]
    item_count = item_columns.shape[1]
    code_count = code_cols.shape[1]
    item_blocks = item_count // BLOCK
    code_blocks = code_count // BLOCK
    logit_scale = 1.0 / (softness_factor * math.sqrt(embedding_width))
    weight_sum = lax.psum(jnp.sum(item_weight), "item")
    capacity_sum = lax.psum(jnp.sum(code_capacity), "code")
    item_logmass = jnp.log(item_weight) - jnp.log(weight_sum)
    code_logmass = jnp.log(code_capacity) - jnp.log(capacity_sum)
    is_live = pairs >= 0
    safe_ids = jnp.where(is_live, pairs, 0)
    target = jnp.where(is_live, pairs, code_blocks)
    item_split_cols = item_columns.reshape(embedding_width, item_blocks, BLOCK)
    code_column_splits = code_cols.reshape(embedding_width, code_blocks, BLOCK)
    group = math.gcd(item_blocks, 8)
    group_count = item_blocks // group

    def build_tiles(own, ids, live):
        picked = code_column_splits[:, ids, :]
        scores = (
            jnp.einsum("rbi,rbsj->bsij", own, picked, precision=lax.Precision.HIGHEST) * logit_scale
        )
        return jnp.where(live[:, :, None, None], scores, masked_score)

    reduce_fn = lambda tiles, ids, portion: tiles

    def one_group(group_index):
        start = group_index * group
        own = lax.dynamic_slice_in_dim(item_split_cols, start, group, 1)
        ids = lax.dynamic_slice_in_dim(safe_ids, start, group, 0)
        live = lax.dynamic_slice_in_dim(is_live, start, group, 0)
        portion = lax.dynamic_slice_in_dim(safe_ids, start, group, 0)
        return reduce_fn(build_tiles(own, ids, live), ids, portion)

    results = lax.map(one_group, jnp.arange(group_count, dtype=jnp.int32))
    saved_tile_blocks = results.reshape((item_blocks,) + results.shape[2:])

    def run_pass(reduce_fn, extra):
        return reduce_fn(saved_tile_blocks, safe_ids, extra)

    flat_target = target.reshape(-1)
    flat_rows = flat_target.shape[0]
    row_group = math.gcd(flat_rows, 256)
    one_hot = flat_target[:, None] == jnp.arange(code_blocks, dtype=jnp.int32)[None, :]
    one_hot_groups = one_hot.reshape(flat_rows // row_group, row_group, code_blocks)
    one_hot_float = one_hot.astype(jnp.float32)
    code_potential = jnp.zeros((code_count,), jnp.float32)
    item_potential = jnp.zeros((item_count,), jnp.float32)
    for sweep in range(ITERS):
        code_split = code_potential.reshape(code_blocks, BLOCK)

        def row_reduce(tiles, ids, portion):
            logits = tiles + code_split[ids][:, :, None, :]
            block_peak = jnp.max(logits, axis=(1, 3))
            block_total = jnp.sum(jnp.exp(logits - block_peak[:, None, :, None]), axis=(1, 3))
            return (block_peak, block_total)

        row_peak, row_total = run_pass(row_reduce, safe_ids)
        row_peak = row_peak.reshape(item_count)
        row_total = row_total.reshape(item_count)
        merged_peak = lax.pmax(row_peak, "code")
        merged_total = lax.psum(row_total * jnp.exp(row_peak - merged_peak), "code")
        item_potential = item_logmass - (merged_peak + jnp.log(merged_total))
        item_split = item_potential.reshape(item_blocks, BLOCK)

        def col_reduce(tiles, ids, portion):
            logits = tiles + portion[:, None, :, None]
            block_peak = jnp.max(logits, axis=2)
            block_total = jnp.sum(jnp.exp(logits - block_peak[:, :, None, :]), axis=2)
            return (block_peak, block_total)

        tile_peak, tile_total = run_pass(col_reduce, item_split)
        peak_flat = tile_peak.reshape(flat_rows, BLOCK)
        total_flat = tile_total.reshape(flat_rows, BLOCK)
        peak_groups = peak_flat.reshape(flat_rows // row_group, row_group, BLOCK)

        def peak_step(carry, pieces):
            hot, peaks = pieces
            candidate = jnp.max(jnp.where(hot[:, :, None], peaks[:, None, :], masked_score), axis=0)
            return (jnp.maximum(carry, candidate), None)

        col_peak, unused = lax.scan(
            peak_step,
            jnp.full((code_blocks, BLOCK), masked_score, jnp.float32),
            (one_hot_groups, peak_groups),
        )
        padded_peak = jnp.concatenate(
            [col_peak, jnp.full((1, BLOCK), masked_score, jnp.float32)], axis=0
        )
        spread = total_flat * jnp.exp(peak_flat - padded_peak[flat_target])
        col_total = jnp.dot(
            one_hot_float.T,
            spread,
            precision=lax.Precision.HIGHEST,
            preferred_element_type=jnp.float32,
        )
        col_peak = col_peak.reshape(code_count)
        col_total = col_total.reshape(code_count)
        joined_peak = lax.pmax(col_peak, "item")
        joined_total = lax.psum(col_total * jnp.exp(col_peak - joined_peak), "item")
        code_potential = code_logmass - (joined_peak + jnp.log(joined_total))
    return (item_potential, code_potential)


def solution(mesh):
    placed = (P("code", "item"), P("item", "code"), P("item"), P("code"), P("item", "code"))
    return jax.shard_map(
        body, mesh=mesh, in_specs=placed, out_specs=(P("item"), P("code")), check_vma=False
    )
```

profile of v0, /device:TPU:0, one launch (start us, length us, event | category | flops | bytes accessed | tf_op | source)
XLA Modules:
  0.0 1095.6 jit_solution(9727637983515556993)
XLA Ops:
  10.0 42.6 %psum.56 = f32[]{:T(128)} all-reduce(f32[]{:T(128)} %reduce_sum.72), channel_id=1, replica_groups=mesh['item'=16,'code'=8] {'item'}, use_global_device_ids=true, to_apply=%region_1.0 | all-reduce | flops 1 | bytes 8 | tf_op jit(solution)/shard_map/psum | solution.py:22
  64.6 52.7 %all-gather.3.cloned.1.call-done = f32[256,8192]{1,0:T(8,128)} async-done(((f32[16,8192]{1,0:T(8,128)}), f32[256,8192]{1,0:T(8,128)}) %all-gather.3.cloned.1.call-update) | async-done | bytes 8388624 | tf_op jit(solution)/shard_map/all_gather | solution.py:15
  126.3 158.7 %while.43 = (s32[]{:T(128)}, f32[8,8,16,64,64]{3,4,2,1,0:T(8,128)}, s32[8]{0:T(128)S(1)}, pred[64,16]{1,0:T(8,128)(4,1)S(1)}, s32[64,16]{1,0:T(8,128)S(1)}, /*in...) while((s32[]{:T(128)}, f32[8,8,16,64,64]{3,4,2,1,0:T(8,128)}, ...), condition=%wide.region_3.0_spmd, body=%wide.region_2.0_spmd.sunk | while | flops 1611662720 | bytes 29892660 | solution.py:51
  155.0 11.0 %bitcast_dynamic-update-slice_fusion.2 = f32[8,8,16,64,64]{3,4,2,1,0:T(8,128)} fusion(f32[8,8,16,64,64]{3,4,2,1,0:T(8,128)} %get-tuple-element.327, s32[]{:T(128)} %get-tuple-element.326, f32[256,8,16,64]{0,3,2,1:T(8,128)} %bitcast.84, pred[8,16]{1,0:T(8,128)(4,1)S(1)} %constant_dynamic-slice_fusion.2, f32[256,64,64]{0,2,1:T(8,128)} %get-tuple-element.343, ...), kind=kOutput, calls=%fused_computation.7.clone.1 | convolution fusion | flops 1611661312 | bytes 13107844 | tf_op jit(solution)/shard_map/while/body/eval_jaxpr/rbi,rbsj->bsij/dot_general | solution.py:37
  234.3 11.0 %bitcast_dynamic-update-slice_fusion.2 = f32[8,8,16,64,64]{3,4,2,1,0:T(8,128)} fusion(f32[8,8,16,64,64]{3,4,2,1,0:T(8,128)} %get-tuple-element.327, s32[]{:T(128)} %get-tuple-element.326, f32[256,8,16,64]{0,3,2,1:T(8,128)} %bitcast.84, pred[8,16]{1,0:T(8,128)(4,1)S(1)} %constant_dynamic-slice_fusion.2, f32[256,64,64]{0,2,1:T(8,128)} %get-tuple-element.343, ...), kind=kOutput, calls=%fused_computation.7.clone.1 | convolution fusion | flops 1611661312 | bytes 13107844 | tf_op jit(solution)/shard_map/while/body/eval_jaxpr/rbi,rbsj->bsij/dot_general | solution.py:37
  285.0 11.8 %add_reduce_fusion.5 = f32[8,8,64]{2,1,0:T(8,128)S(1)} fusion(f32[8,8,16,64,64]{3,4,2,1,0:T(8,128)} %get-tuple-element.105, f32[8,8,16,64]{3,2,1,0:T(8,128)S(1)} %bitcast.93), kind=kLoop, calls=%fused_computation.37 | loop fusion | flops 8384512 | bytes 17055744 | tf_op jit(solution)/shard_map/reduce_max | solution.py:70
  296.8 11.9 %exponential_reduce_fusion.5 = f32[8,8,64]{2,1,0:T(8,128)S(1)} fusion(f32[8,8,16,64,64]{3,4,2,1,0:T(8,128)} %get-tuple-element.105, f32[8,8,64]{2,1,0:T(8,128)S(1)} %add_reduce_fusion.5, f32[8,8,16,64]{3,2,1,0:T(8,128)S(1)} %bitcast.94), kind=kLoop, calls=%fused_computation.31 | loop fusion | flops 12578816 | bytes 17072128 | tf_op jit(solution)/shard_map/reduce_sum | solution.py:71
  308.9 25.5 %pmax.42 = f32[4096]{0:T(1024)S(1)} all-reduce(f32[4096]{0:T(1024)S(1)} %reshape.211), channel_id=1, replica_groups=mesh['item'=16,'code'=8] {'code'}, use_global_device_ids=true, to_apply=%region_7.8 | all-reduce | flops 4096 | bytes 32768 | tf_op jit(solution)/shard_map/pmax | solution.py:77
  334.4 24.6 %all-reduce.3 = (f32[4096]{0:T(1024)S(1)}, f32[]{:T(128)}) all-reduce(f32[4096]{0:T(1024)S(1)} %exponential_multiply_fusion.5, f32[]{:T(128)} %reduce_sum.73), channel_id=1, replica_groups=mesh['item'=16,'code'=8] {'code'}, use_global_device_ids=true, to_apply=%region_9.10 | all-reduce | flops 4097 | bytes 32776 | tf_op jit(solution)/shard_map/psum | solution.py:78
  359.1 15.3 %add_reduce_fusion.4 = f32[8,8,16,64]{3,2,1,0:T(8,128)S(1)} fusion(f32[8,8,16,64,64]{3,4,2,1,0:T(8,128)} %get-tuple-element.105, f32[8,8,64]{2,1,0:T(8,128)S(1)} %add.154), kind=kLoop, calls=%fused_computation.36 | loop fusion | flops 8323072 | bytes 17055744 | tf_op jit(solution)/shard_map/reduce_max | solution.py:84
  374.4 20.7 %exponential_reduce_fusion.4 = f32[8,8,16,64]{3,2,1,0:T(8,128)S(1)} fusion(f32[8,8,16,64,64]{3,4,2,1,0:T(8,128)} %get-tuple-element.105, f32[8,8,16,64]{3,2,1,0:T(8,128)S(1)} %add_reduce_fusion.4, f32[8,8,64]{2,1,0:T(8,128)S(1)} %add.154), kind=kLoop, calls=%fused_computation.30 | loop fusion | flops 12517376 | bytes 17317888 | tf_op jit(solution)/shard_map/reduce_sum | solution.py:85
  395.1 13.3 %while.44 = (s32[]{:T(128)}, f32[128,64]{0,1:T(8,128)S(1)}, pred[4,256,128]{2,1,0:T(8,128)(4,1)S(1)}, f32[4,256,64]{2,1,0:T(8,128)S(1)}, s32[]{:T(128)}, /*index=5*/s32[]{:T(128)}) while((s32[]{:T(128)}, f32[128,64]{0,1:T(8,128)S(1)}, pred[4,256,128]{2,1,0:T(8,128)(4,1)S(1)}, f32[4,256,64]{2,1,0:T(8,128)S(1)}, s32[]{:T(128)}, ...), condition=%wide.region_13.14_spmd.clone, body=%wide.region_11.13_spmd.clone.sunk | while | flops 4202499 | bytes 426071 | solution.py:98
  412.4 72.4 %pmax.43 = f32[8192]{0:T(1024)S(1)} all-reduce(f32[8192]{0:T(1024)S(1)} %reshape.213), channel_id=1, replica_groups=mesh['item'=16,'code'=8] {'item'}, use_global_device_ids=true, to_apply=%region_14.15 | all-reduce | flops 8192 | bytes 65536 | tf_op jit(solution)/shard_map/pmax | solution.py:115
  484.8 69.5 %psum.59 = f32[8192]{0:T(1024)S(1)} all-reduce(f32[8192]{0:T(1024)S(1)} %exponential_multiply_fusion.2), channel_id=1, replica_groups=mesh['item'=16,'code'=8] {'item'}, use_global_device_ids=true, to_apply=%region_16.17 | all-reduce | flops 8192 | bytes 65536 | tf_op jit(solution)/shard_map/psum | solution.py:116
  558.0 11.8 %add_reduce_fusion.3 = f32[8,8,64]{2,1,0:T(8,128)S(1)} fusion(f32[8,8,16,64,64]{3,4,2,1,0:T(8,128)} %get-tuple-element.105, f32[8,8,16,64]{3,2,1,0:T(8,128)S(1)} %bitcast.97), kind=kLoop, calls=%fused_computation.35 | loop fusion | flops 8384512 | bytes 17055744 | tf_op jit(solution)/shard_map/reduce_max | solution.py:70
  569.8 11.9 %exponential_reduce_fusion.3 = f32[8,8,64]{2,1,0:T(8,128)S(1)} fusion(f32[8,8,16,64,64]{3,4,2,1,0:T(8,128)} %get-tuple-element.105, f32[8,8,64]{2,1,0:T(8,128)S(1)} %add_reduce_fusion.3, f32[8,8,16,64]{3,2,1,0:T(8,128)S(1)} %bitcast.98), kind=kLoop, calls=%fused_computation.29 | loop fusion | flops 12578816 | bytes 17072128 | tf_op jit(solution)/shard_map/reduce_sum | solution.py:71
  581.9 23.5 %pmax.44 = f32[4096]{0:T(1024)S(1)} all-reduce(f32[4096]{0:T(1024)S(1)} %reshape.219), channel_id=1, replica_groups=mesh['item'=16,'code'=8] {'code'}, use_global_device_ids=true, to_apply=%region_18.19 | all-reduce | flops 4096 | bytes 32768 | tf_op jit(solution)/shard_map/pmax | solution.py:77
  605.4 23.6 %psum.60 = f32[4096]{0:T(1024)S(1)} all-reduce(f32[4096]{0:T(1024)S(1)} %exponential_multiply_fusion.4), channel_id=1, replica_groups=mesh['item'=16,'code'=8] {'code'}, use_global_device_ids=true, to_apply=%region_20.21 | all-reduce | flops 4096 | bytes 32768 | tf_op jit(solution)/shard_map/psum | solution.py:78
  629.1 15.3 %add_reduce_fusion.2 = f32[8,8,16,64]{3,2,1,0:T(8,128)S(1)} fusion(f32[8,8,16,64,64]{3,4,2,1,0:T(8,128)} %get-tuple-element.105, f32[8,8,64]{2,1,0:T(8,128)S(1)} %add.163), kind=kLoop, calls=%fused_computation.34 | loop fusion | flops 8323072 | bytes 17055744 | tf_op jit(solution)/shard_map/reduce_max | solution.py:84
  644.4 20.7 %exponential_reduce_fusion.2 = f32[8,8,16,64]{3,2,1,0:T(8,128)S(1)} fusion(f32[8,8,16,64,64]{3,4,2,1,0:T(8,128)} %get-tuple-element.105, f32[8,8,16,64]{3,2,1,0:T(8,128)S(1)} %add_reduce_fusion.2, f32[8,8,64]{2,1,0:T(8,128)S(1)} %add.163), kind=kLoop, calls=%fused_computation.28 | loop fusion | flops 12517376 | bytes 17317888 | tf_op jit(solution)/shard_map/reduce_sum | solution.py:85
  665.0 13.3 %while.45 = (s32[]{:T(128)}, f32[128,64]{0,1:T(8,128)S(1)}, pred[4,256,128]{2,1,0:T(8,128)(4,1)S(1)}, f32[4,256,64]{2,1,0:T(8,128)S(1)}, s32[]{:T(128)}, /*index=5*/s32[]{:T(128)}) while((s32[]{:T(128)}, f32[128,64]{0,1:T(8,128)S(1)}, pred[4,256,128]{2,1,0:T(8,128)(4,1)S(1)}, f32[4,256,64]{2,1,0:T(8,128)S(1)}, s32[]{:T(128)}, ...), condition=%wide.region_24.25_spmd.clone, body=%wide.region_22.24_spmd.clone.sunk | while | flops 4202499 | bytes 426071 | solution.py:98
  682.3 69.6 %pmax.45 = f32[8192]{0:T(1024)S(1)} all-reduce(f32[8192]{0:T(1024)S(1)} %reshape.221), channel_id=1, replica_groups=mesh['item'=16,'code'=8] {'item'}, use_global_device_ids=true, to_apply=%region_25.26 | all-reduce | flops 8192 | bytes 65536 | tf_op jit(solution)/shard_map/pmax | solution.py:115
  751.9 69.5 %psum.61 = f32[8192]{0:T(1024)S(1)} all-reduce(f32[8192]{0:T(1024)S(1)} %exponential_multiply_fusion.1), channel_id=1, replica_groups=mesh['item'=16,'code'=8] {'item'}, use_global_device_ids=true, to_apply=%region_27.28 | all-reduce | flops 8192 | bytes 65536 | tf_op jit(solution)/shard_map/psum | solution.py:116
  824.4 11.8 %add_reduce_fusion.1 = f32[8,8,64]{2,1,0:T(8,128)S(1)} fusion(f32[8,8,16,64,64]{3,4,2,1,0:T(8,128)} %get-tuple-element.105, f32[8,8,16,64]{3,2,1,0:T(8,128)S(1)} %bitcast.95), kind=kLoop, calls=%fused_computation.33 | loop fusion | flops 8384512 | bytes 17055744 | tf_op jit(solution)/shard_map/reduce_max | solution.py:70
  836.2 11.9 %exponential_reduce_fusion.1 = f32[8,8,64]{2,1,0:T(8,128)S(1)} fusion(f32[8,8,16,64,64]{3,4,2,1,0:T(8,128)} %get-tuple-element.105, f32[8,8,64]{2,1,0:T(8,128)S(1)} %add_reduce_fusion.1, f32[8,8,16,64]{3,2,1,0:T(8,128)S(1)} %bitcast.96), kind=kLoop, calls=%fused_computation.27 | loop fusion | flops 12578816 | bytes 17072128 | tf_op jit(solution)/shard_map/reduce_sum | solution.py:71
  848.3 23.5 %pmax.46 = f32[4096]{0:T(1024)S(1)} all-reduce(f32[4096]{0:T(1024)S(1)} %reshape.226), channel_id=1, replica_groups=mesh['item'=16,'code'=8] {'code'}, use_global_device_ids=true, to_apply=%region_29.30 | all-reduce | flops 4096 | bytes 32768 | tf_op jit(solution)/shard_map/pmax | solution.py:77
  871.8 23.8 %psum.62 = f32[4096]{0:T(1024)S(1)} all-reduce(f32[4096]{0:T(1024)S(1)} %exponential_multiply_fusion.3), channel_id=1, replica_groups=mesh['item'=16,'code'=8] {'code'}, use_global_device_ids=true, to_apply=%region_31.32 | all-reduce | flops 4096 | bytes 32768 | tf_op jit(solution)/shard_map/psum | solution.py:78
  895.7 15.3 %add_reduce_fusion = f32[8,8,16,64]{3,2,1,0:T(8,128)S(1)} fusion(f32[8,8,16,64,64]{3,4,2,1,0:T(8,128)} %get-tuple-element.105, f32[8,8,64]{2,1,0:T(8,128)S(1)} %add.171), kind=kLoop, calls=%fused_computation.32 | loop fusion | flops 8323072 | bytes 17055744 | tf_op jit(solution)/shard_map/reduce_max | solution.py:84
  911.0 20.7 %exponential_reduce_fusion = f32[8,8,16,64]{3,2,1,0:T(8,128)S(1)} fusion(f32[8,8,16,64,64]{3,4,2,1,0:T(8,128)} %get-tuple-element.105, f32[8,8,16,64]{3,2,1,0:T(8,128)S(1)} %add_reduce_fusion, f32[8,8,64]{2,1,0:T(8,128)S(1)} %add.171), kind=kLoop, calls=%fused_computation.26 | loop fusion | flops 12517376 | bytes 17317888 | tf_op jit(solution)/shard_map/reduce_sum | solution.py:85
  931.7 13.3 %while.46 = (s32[]{:T(128)}, f32[128,64]{0,1:T(8,128)S(1)}, pred[4,256,128]{2,1,0:T(8,128)(4,1)S(1)}, f32[4,256,64]{2,1,0:T(8,128)S(1)}, s32[]{:T(128)}, /*index=5*/s32[]{:T(128)}) while((s32[]{:T(128)}, f32[128,64]{0,1:T(8,128)S(1)}, pred[4,256,128]{2,1,0:T(8,128)(4,1)S(1)}, f32[4,256,64]{2,1,0:T(8,128)S(1)}, s32[]{:T(128)}, ...), condition=%wide.region_35.36_spmd.clone, body=%wide.region_33.35_spmd.clone.sunk | while | flops 4202499 | bytes 426071 | solution.py:98
  948.9 69.6 %pmax.47 = f32[8192]{0:T(1024)S(1)} all-reduce(f32[8192]{0:T(1024)S(1)} %reshape.228), channel_id=1, replica_groups=mesh['item'=16,'code'=8] {'item'}, use_global_device_ids=true, to_apply=%region_36.37 | all-reduce | flops 8192 | bytes 65536 | tf_op jit(solution)/shard_map/pmax | solution.py:115
  1018.5 69.5 %psum.63 = f32[8192]{0:T(1024)S(1)} all-reduce(f32[8192]{0:T(1024)S(1)} %exponential_multiply_fusion), channel_id=1, replica_groups=mesh['item'=16,'code'=8] {'item'}, use_global_device_ids=true, to_apply=%region_38.39 | all-reduce | flops 8192 | bytes 65536 | tf_op jit(solution)/shard_map/psum | solution.py:116
  (185 shorter events, 213.5 us)
Async XLA Ops:
  7.2 51.8 %all-gather.5.cloned.1.call-start = ((), (), s32[]{:S(2)}) async-start(), calls=%async_computation.1 | async-start | bytes 4718592 | tf_op jit(solution)/shard_map/all_gather | solution.py:14
  7.9 109.4 %all-gather.3.cloned.1.call-start = ((), (), s32[]{:S(2)}) async-start(), calls=%async_computation | async-start | bytes 8912896 | tf_op jit(solution)/shard_map/all_gather | solution.py:15
  285.0 74.0 %copy-start.3 = (f32[4096]{0:T(1024)S(1)}, f32[4096]{0:T(1024)}, u32[]{:S(2)}) copy-start(f32[4096]{0:T(1024)} %param.15) | copy-start | bytes 49156
  359.1 195.9 %copy-start.2 = (f32[8192]{0:T(1024)S(1)}, f32[8192]{0:T(1024)}, u32[]{:S(2)}) copy-start(f32[8192]{0:T(1024)} %param.16) | copy-start | bytes 98308
  629.1 36.0 %copy-start.1 = (f32[128,64]{0,1:T(8,128)S(1)}, f32[128,64]{0,1:T(8,128)}, u32[]{:S(2)}) copy-start(f32[128,64]{0,1:T(8,128)} %custom-call.1) | copy-start | bytes 98308
  895.6 36.1 %copy-start.4 = (f32[4096]{0:T(1024)}, f32[4096]{0:T(1024)S(1)}, u32[]{:S(2)}) copy-start(f32[4096]{0:T(1024)S(1)} %add_subtract_fusion.3) | copy-start | bytes 49156
  895.7 36.0 %copy-start = (f32[128,64]{0,1:T(8,128)S(1)}, f32[128,64]{0,1:T(8,128)}, u32[]{:S(2)}) copy-start(f32[128,64]{0,1:T(8,128)} %custom-call.2) | copy-start | bytes 98308
Sparse Core Ops, SparseCore 0:
  9.7 34.5 all-gather.4
  46.4 70.8 all-gather.2
where the time goes:
time: 1100 us
  blocking collectives  607 us (55%)
  other arithmetic  222 us (20%)
  local copies, waits for them, and re-layouts  101 us (9%)
  matrix products  89.9 us (8%)
  waiting for transfers between devices  54.1 us (5%)
  between operations  15.8 us (1%)
    pmax x3, blocking collectives, body(): joined_peak = lax.pmax(col_peak, 'item')  212 us
    psum x3, blocking collectives, body(): joined_total = lax.psum(col_total * jnp.exp(col_peak - joined_peak), 'item')  209 us
    dot_general x8, matrix products, build_tiles(): jnp.einsum('rbi,rbsj->bsij', own, picked, precision=lax.Precision.HIGHEST)  87.6 us
    pmax x3, blocking collectives, body(): merged_peak = lax.pmax(row_peak, 'code')  72.6 us
    psum x3, blocking collectives, body(): merged_total = lax.psum(row_total * jnp.exp(row_peak - merged_peak), 'code')  71.9 us
    reduce_sum x3, other arithmetic, col_reduce(): block_total = jnp.sum(jnp.exp(logits - block_peak[:, :, None, :]), axis=2)  62 us
    gather x8, local copies, waits for them, and re-layouts, build_tiles(): picked = code_column_splits[:, ids, :]  61.3 us
    all_gather x1, waiting for transfers between devices, body(): code_cols = lax.all_gather(codebook, 'item', axis=0, tiled=True)  52.7 us
  transfers between devices with their start and end apart: 2, of which 1 were waited for; matrix products, arithmetic and copies ran while one was open for 1% of the time, Pallas kernels for 0%

commit v1 on v0

--- a/solution.py
+++ b/solution.py
@@ -12,7 +12,9 @@
 
 def body(residuals, codebook, item_weight, code_capacity, pairs):
     item_columns = lax.all_gather(residuals, "code", axis=0, tiled=True)
-    code_cols = lax.all_gather(codebook, "item", axis=0, tiled=True)
+    code_cols = jnp.concatenate(
+        lax.all_to_all(jnp.stack([codebook] * lax.axis_size("item")), "item", 0, 0), axis=0
+    )
     embedding_width = item_columns.shape[0]
     item_count = item_columns.shape[1]
     code_count = code_cols.shape[1]

time: 1100 us -> 1180 us (1.073)
  blocking collectives: 607 us -> 711 us
  waiting for transfers between devices: 54.1 us -> 0.7 us
  local copies, waits for them, and re-layouts: 101 us -> 126 us
    psum x1, blocking collectives: 42.6 us -> 150 us  [body(): weight_sum = lax.psum(jnp.sum(item_weight), 'item')]
    all_gather x1 -> x0, waiting for transfers between devices: 52.7 us -> none  [body(): code_cols = lax.all_gather(codebook, 'item', axis=0, tiled=True)]
    another operation x0 -> x2, local copies, waits for them, and re-layouts: none -> 19.4 us  [the longest x1 14.2 us: body(): code_column_splits = code_cols.reshape(embedding_width, code_blocks, BLOCK)]
    while x0 -> x1, local copies, waits for them, and re-layouts: none -> 14.1 us  [body(): results = lax.map(one_group, jnp.arange(group_count, dtype=jnp.int32))]
  transfers between devices with their start and end apart: 2 -> 2, of which waited for: 1 -> 0; matrix products, arithmetic and copies ran while one was open for 1% -> 1% of each run, Pallas kernels for 0% -> 0%
where the time goes in v1:
time: 1180 us
  blocking collectives  711 us (60%)
  other arithmetic  222 us (19%)
  local copies, waits for them, and re-layouts  126 us (11%)
  matrix products  89.9 us (8%)
  between operations  15.8 us (1%)
    pmax x3, blocking collectives, body(): joined_peak = lax.pmax(col_peak, 'item')  209 us
    psum x3, blocking collectives, body(): joined_total = lax.psum(col_total * jnp.exp(col_peak - joined_peak), 'item')  209 us
    psum x1, blocking collectives, body(): weight_sum = lax.psum(jnp.sum(item_weight), 'item')  150 us
    dot_general x8, matrix products, build_tiles(): jnp.einsum('rbi,rbsj->bsij', own, picked, precision=lax.Precision.HIGHEST)  87.6 us
    psum x3, blocking collectives, body(): merged_total = lax.psum(row_total * jnp.exp(row_peak - merged_peak), 'code')  71.8 us
    pmax x3, blocking collectives, body(): merged_peak = lax.pmax(row_peak, 'code')  70.6 us
    reduce_sum x3, other arithmetic, col_reduce(): block_total = jnp.sum(jnp.exp(logits - block_peak[:, :, None, :]), axis=2)  62 us
    gather x8, local copies, waits for them, and re-layouts, build_tiles(): picked = code_column_splits[:, ids, :]  61.3 us
  transfers between devices with their start and end apart: 2, of which 0 were waited for; matrix products, arithmetic and copies ran while one was open for 1% of the time, Pallas kernels for 0%

profile of v1, /device:TPU:0, one launch (start us, length us, event | category | flops | bytes accessed | tf_op | source)
XLA Modules:
  0.0 1179.8 jit_solution(9077025002918147832)
XLA Ops:
  22.6 150.3 %psum.56 = f32[]{:T(128)} all-reduce(f32[]{:T(128)} %reduce_sum.72), channel_id=1, replica_groups=mesh['item'=16,'code'=8] {'item'}, use_global_device_ids=true, to_apply=%region_1.0 | all-reduce | flops 1 | bytes 8 | tf_op jit(solution)/shard_map/psum | solution.py:24
  184.8 14.2 %reshape_reshape.12 = f32[256,128,64]{2,1,0:T(8,128)} reshape(f32[16,16,8192]{2,1,0:T(8,128)} %all-to-all-done) | data formatting | bytes 16777216 | tf_op jit(solution)/shard_map/reshape;reshape | solution.py:32
  199.0 14.1 %copy.23 = f32[256,128,64]{0,2,1:T(8,128)} copy(f32[256,128,64]{2,1,0:T(8,128)} %reshape_reshape.12) | data formatting | bytes 16777216 | tf_op jit(solution)/shard_map/while | solution.py:53
  213.1 160.4 %while.43 = (s32[]{:T(128)}, f32[8,8,16,64,64]{3,4,2,1,0:T(8,128)}, s32[8]{0:T(128)S(1)}, pred[64,16]{1,0:T(8,128)(4,1)S(1)}, s32[64,16]{1,0:T(8,128)S(1)}, /*in...) while((s32[]{:T(128)}, f32[8,8,16,64,64]{3,4,2,1,0:T(8,128)}, ...), condition=%wide.region_3.0_spmd, body=%wide.region_2.0_spmd.sunk | while | flops 1611662720 | bytes 29892660 | solution.py:53
  242.2 11.0 bitcast_dynamic-update-slice_fusion.2
  373.5 11.8 %add_reduce_fusion.5 = f32[8,8,64]{2,1,0:T(8,128)S(1)} fusion(f32[8,8,16,64,64]{3,4,2,1,0:T(8,128)} %get-tuple-element.105, f32[8,8,16,64]{3,2,1,0:T(8,128)S(1)} %bitcast.91), kind=kLoop, calls=%fused_computation.37 | loop fusion | flops 8384512 | bytes 17055744 | tf_op jit(solution)/shard_map/reduce_max | solution.py:72
  385.3 11.9 %exponential_reduce_fusion.5 = f32[8,8,64]{2,1,0:T(8,128)S(1)} fusion(f32[8,8,16,64,64]{3,4,2,1,0:T(8,128)} %get-tuple-element.105, f32[8,8,64]{2,1,0:T(8,128)S(1)} %add_reduce_fusion.5, f32[8,8,16,64]{3,2,1,0:T(8,128)S(1)} %bitcast.92), kind=kLoop, calls=%fused_computation.31 | loop fusion | flops 12578816 | bytes 17072128 | tf_op jit(solution)/shard_map/reduce_sum | solution.py:73
  397.4 23.5 %pmax.42 = f32[4096]{0:T(1024)S(1)} all-reduce(f32[4096]{0:T(1024)S(1)} %reshape.209), channel_id=1, replica_groups=mesh['item'=16,'code'=8] {'code'}, use_global_device_ids=true, to_apply=%region_7.8 | all-reduce | flops 4096 | bytes 32768 | tf_op jit(solution)/shard_map/pmax | solution.py:79
  421.0 24.7 %all-reduce.3 = (f32[4096]{0:T(1024)S(1)}, f32[]{:T(128)}) all-reduce(f32[4096]{0:T(1024)S(1)} %exponential_multiply_fusion.5, f32[]{:T(128)} %reduce_sum.73), channel_id=1, replica_groups=mesh['item'=16,'code'=8] {'code'}, use_global_device_ids=true, to_apply=%region_9.10 | all-reduce | flops 4097 | bytes 32776 | tf_op jit(solution)/shard_map/psum | solution.py:80
  445.8 15.3 %add_reduce_fusion.4 = f32[8,8,16,64]{3,2,1,0:T(8,128)S(1)} fusion(f32[8,8,16,64,64]{3,4,2,1,0:T(8,128)} %get-tuple-element.105, f32[8,8,64]{2,1,0:T(8,128)S(1)} %add.154), kind=kLoop, calls=%fused_computation.36 | loop fusion | flops 8323072 | bytes 17055744 | tf_op jit(solution)/shard_map/reduce_max | solution.py:86
  461.1 20.7 %exponential_reduce_fusion.4 = f32[8,8,16,64]{3,2,1,0:T(8,128)S(1)} fusion(f32[8,8,16,64,64]{3,4,2,1,0:T(8,128)} %get-tuple-element.105, f32[8,8,16,64]{3,2,1,0:T(8,128)S(1)} %add_reduce_fusion.4, f32[8,8,64]{2,1,0:T(8,128)S(1)} %add.154), kind=kLoop, calls=%fused_computation.30 | loop fusion | flops 12517376 | bytes 17317888 | tf_op jit(solution)/shard_map/reduce_sum | solution.py:87
  481.7 13.3 %while.44 = (s32[]{:T(128)}, f32[128,64]{0,1:T(8,128)S(1)}, pred[4,256,128]{2,1,0:T(8,128)(4,1)S(1)}, f32[4,256,64]{2,1,0:T(8,128)S(1)}, s32[]{:T(128)}, /*index=5*/s32[]{:T(128)}) while((s32[]{:T(128)}, f32[128,64]{0,1:T(8,128)S(1)}, pred[4,256,128]{2,1,0:T(8,128)(4,1)S(1)}, f32[4,256,64]{2,1,0:T(8,128)S(1)}, s32[]{:T(128)}, ...), condition=%wide.region_13.14_spmd.clone, body=%wide.region_11.13_spmd.clone.sunk | while | flops 4202499 | bytes 426071 | solution.py:100
  499.0 70.0 %pmax.43 = f32[8192]{0:T(1024)S(1)} all-reduce(f32[8192]{0:T(1024)S(1)} %reshape.211), channel_id=1, replica_groups=mesh['item'=16,'code'=8] {'item'}, use_global_device_ids=true, to_apply=%region_14.15 | all-reduce | flops 8192 | bytes 65536 | tf_op jit(solution)/shard_map/pmax | solution.py:117
  569.1 69.5 %psum.59 = f32[8192]{0:T(1024)S(1)} all-reduce(f32[8192]{0:T(1024)S(1)} %exponential_multiply_fusion.2), channel_id=1, replica_groups=mesh['item'=16,'code'=8] {'item'}, use_global_device_ids=true, to_apply=%region_16.17 | all-reduce | flops 8192 | bytes 65536 | tf_op jit(solution)/shard_map/psum | solution.py:118
  642.2 11.8 %add_reduce_fusion.3 = f32[8,8,64]{2,1,0:T(8,128)S(1)} fusion(f32[8,8,16,64,64]{3,4,2,1,0:T(8,128)} %get-tuple-element.105, f32[8,8,16,64]{3,2,1,0:T(8,128)S(1)} %bitcast.95), kind=kLoop, calls=%fused_computation.35 | loop fusion | flops 8384512 | bytes 17055744 | tf_op jit(solution)/shard_map/reduce_max | solution.py:72
  654.0 11.9 %exponential_reduce_fusion.3 = f32[8,8,64]{2,1,0:T(8,128)S(1)} fusion(f32[8,8,16,64,64]{3,4,2,1,0:T(8,128)} %get-tuple-element.105, f32[8,8,64]{2,1,0:T(8,128)S(1)} %add_reduce_fusion.3, f32[8,8,16,64]{3,2,1,0:T(8,128)S(1)} %bitcast.96), kind=kLoop, calls=%fused_computation.29 | loop fusion | flops 12578816 | bytes 17072128 | tf_op jit(solution)/shard_map/reduce_sum | solution.py:73
  666.1 23.5 %pmax.44 = f32[4096]{0:T(1024)S(1)} all-reduce(f32[4096]{0:T(1024)S(1)} %reshape.217), channel_id=1, replica_groups=mesh['item'=16,'code'=8] {'code'}, use_global_device_ids=true, to_apply=%region_18.19 | all-reduce | flops 4096 | bytes 32768 | tf_op jit(solution)/shard_map/pmax | solution.py:79
  689.7 23.6 %psum.60 = f32[4096]{0:T(1024)S(1)} all-reduce(f32[4096]{0:T(1024)S(1)} %exponential_multiply_fusion.4), channel_id=1, replica_groups=mesh['item'=16,'code'=8] {'code'}, use_global_device_ids=true, to_apply=%region_20.21 | all-reduce | flops 4096 | bytes 32768 | tf_op jit(solution)/shard_map/psum | solution.py:80
  713.3 15.3 %add_reduce_fusion.2 = f32[8,8,16,64]{3,2,1,0:T(8,128)S(1)} fusion(f32[8,8,16,64,64]{3,4,2,1,0:T(8,128)} %get-tuple-element.105, f32[8,8,64]{2,1,0:T(8,128)S(1)} %add.163), kind=kLoop, calls=%fused_computation.34 | loop fusion | flops 8323072 | bytes 17055744 | tf_op jit(solution)/shard_map/reduce_max | solution.py:86
  728.6 20.7 %exponential_reduce_fusion.2 = f32[8,8,16,64]{3,2,1,0:T(8,128)S(1)} fusion(f32[8,8,16,64,64]{3,4,2,1,0:T(8,128)} %get-tuple-element.105, f32[8,8,16,64]{3,2,1,0:T(8,128)S(1)} %add_reduce_fusion.2, f32[8,8,64]{2,1,0:T(8,128)S(1)} %add.163), kind=kLoop, calls=%fused_computation.28 | loop fusion | flops 12517376 | bytes 17317888 | tf_op jit(solution)/shard_map/reduce_sum | solution.py:87
  749.3 13.3 %while.45 = (s32[]{:T(128)}, f32[128,64]{0,1:T(8,128)S(1)}, pred[4,256,128]{2,1,0:T(8,128)(4,1)S(1)}, f32[4,256,64]{2,1,0:T(8,128)S(1)}, s32[]{:T(128)}, /*index=5*/s32[]{:T(128)}) while((s32[]{:T(128)}, f32[128,64]{0,1:T(8,128)S(1)}, pred[4,256,128]{2,1,0:T(8,128)(4,1)S(1)}, f32[4,256,64]{2,1,0:T(8,128)S(1)}, s32[]{:T(128)}, ...), condition=%wide.region_24.25_spmd.clone, body=%wide.region_22.24_spmd.clone.sunk | while | flops 4202499 | bytes 426071 | solution.py:100
  766.6 69.5 %pmax.45 = f32[8192]{0:T(1024)S(1)} all-reduce(f32[8192]{0:T(1024)S(1)} %reshape.219), channel_id=1, replica_groups=mesh['item'=16,'code'=8] {'item'}, use_global_device_ids=true, to_apply=%region_25.26 | all-reduce | flops 8192 | bytes 65536 | tf_op jit(solution)/shard_map/pmax | solution.py:117
  836.1 69.8 %psum.61 = f32[8192]{0:T(1024)S(1)} all-reduce(f32[8192]{0:T(1024)S(1)} %exponential_multiply_fusion.1), channel_id=1, replica_groups=mesh['item'=16,'code'=8] {'item'}, use_global_device_ids=true, to_apply=%region_27.28 | all-reduce | flops 8192 | bytes 65536 | tf_op jit(solution)/shard_map/psum | solution.py:118
  908.8 11.8 %add_reduce_fusion.1 = f32[8,8,64]{2,1,0:T(8,128)S(1)} fusion(f32[8,8,16,64,64]{3,4,2,1,0:T(8,128)} %get-tuple-element.105, f32[8,8,16,64]{3,2,1,0:T(8,128)S(1)} %bitcast.93), kind=kLoop, calls=%fused_computation.33 | loop fusion | flops 8384512 | bytes 17055744 | tf_op jit(solution)/shard_map/reduce_max | solution.py:72
  920.6 11.9 %exponential_reduce_fusion.1 = f32[8,8,64]{2,1,0:T(8,128)S(1)} fusion(f32[8,8,16,64,64]{3,4,2,1,0:T(8,128)} %get-tuple-element.105, f32[8,8,64]{2,1,0:T(8,128)S(1)} %add_reduce_fusion.1, f32[8,8,16,64]{3,2,1,0:T(8,128)S(1)} %bitcast.94), kind=kLoop, calls=%fused_computation.27 | loop fusion | flops 12578816 | bytes 17072128 | tf_op jit(solution)/shard_map/reduce_sum | solution.py:73
  932.7 23.5 %pmax.46 = f32[4096]{0:T(1024)S(1)} all-reduce(f32[4096]{0:T(1024)S(1)} %reshape.224), channel_id=1, replica_groups=mesh['item'=16,'code'=8] {'code'}, use_global_device_ids=true, to_apply=%region_29.30 | all-reduce | flops 4096 | bytes 32768 | tf_op jit(solution)/shard_map/pmax | solution.py:79
  956.2 23.6 %psum.62 = f32[4096]{0:T(1024)S(1)} all-reduce(f32[4096]{0:T(1024)S(1)} %exponential_multiply_fusion.3), channel_id=1, replica_groups=mesh['item'=16,'code'=8] {'code'}, use_global_device_ids=true, to_apply=%region_31.32 | all-reduce | flops 4096 | bytes 32768 | tf_op jit(solution)/shard_map/psum | solution.py:80
  979.9 15.3 %add_reduce_fusion = f32[8,8,16,64]{3,2,1,0:T(8,128)S(1)} fusion(f32[8,8,16,64,64]{3,4,2,1,0:T(8,128)} %get-tuple-element.105, f32[8,8,64]{2,1,0:T(8,128)S(1)} %add.171), kind=kLoop, calls=%fused_computation.32 | loop fusion | flops 8323072 | bytes 17055744 | tf_op jit(solution)/shard_map/reduce_max | solution.py:86
  995.2 20.7 %exponential_reduce_fusion = f32[8,8,16,64]{3,2,1,0:T(8,128)S(1)} fusion(f32[8,8,16,64,64]{3,4,2,1,0:T(8,128)} %get-tuple-element.105, f32[8,8,16,64]{3,2,1,0:T(8,128)S(1)} %add_reduce_fusion, f32[8,8,64]{2,1,0:T(8,128)S(1)} %add.171), kind=kLoop, calls=%fused_computation.26 | loop fusion | flops 12517376 | bytes 17317888 | tf_op jit(solution)/shard_map/reduce_sum | solution.py:87
  1015.9 13.3 %while.46 = (s32[]{:T(128)}, f32[128,64]{0,1:T(8,128)S(1)}, pred[4,256,128]{2,1,0:T(8,128)(4,1)S(1)}, f32[4,256,64]{2,1,0:T(8,128)S(1)}, s32[]{:T(128)}, /*index=5*/s32[]{:T(128)}) while((s32[]{:T(128)}, f32[128,64]{0,1:T(8,128)S(1)}, pred[4,256,128]{2,1,0:T(8,128)(4,1)S(1)}, f32[4,256,64]{2,1,0:T(8,128)S(1)}, s32[]{:T(128)}, ...), condition=%wide.region_35.36_spmd.clone, body=%wide.region_33.35_spmd.clone.sunk | while | flops 4202499 | bytes 426071 | solution.py:100
  1033.2 69.6 %pmax.47 = f32[8192]{0:T(1024)S(1)} all-reduce(f32[8192]{0:T(1024)S(1)} %reshape.226), channel_id=1, replica_groups=mesh['item'=16,'code'=8] {'item'}, use_global_device_ids=true, to_apply=%region_36.37 | all-reduce | flops 8192 | bytes 65536 | tf_op jit(solution)/shard_map/pmax | solution.py:117
  1102.7 69.5 %psum.63 = f32[8192]{0:T(1024)S(1)} all-reduce(f32[8192]{0:T(1024)S(1)} %exponential_multiply_fusion), channel_id=1, replica_groups=mesh['item'=16,'code'=8] {'item'}, use_global_device_ids=true, to_apply=%region_38.39 | all-reduce | flops 8192 | bytes 65536 | tf_op jit(solution)/shard_map/psum | solution.py:118
  (186 shorter events, 228.8 us)
Async XLA Ops:
  12.4 172.5 %all-to-all-start = ((f32[16,16,8192]{2,1,0:T(8,128)}), f32[16,16,8192]{2,1,0:T(8,128)}, u32[]{:S(2)}, u32[]{:S(2)}) async-start(f32[16,16,8192]{2,1,0:T(8,128)} %stack.2), calls=%async_computation | async-start | bytes 16777216 | tf_op jit(solution)/shard_map/all_to_all | solution.py:16
  20.6 158.7 %all-gather.2.cloned.1.call-start = ((), (), s32[]{:S(2)}) async-start(), calls=%async_computation.1 | async-start | bytes 4718592 | tf_op jit(solution)/shard_map/all_gather | solution.py:14
  373.5 72.2 %copy-start.3 = (f32[4096]{0:T(1024)S(1)}, f32[4096]{0:T(1024)}, u32[]{:S(2)}) copy-start(f32[4096]{0:T(1024)} %param.15) | copy-start | bytes 49156
  445.8 193.5 %copy-start.2 = (f32[8192]{0:T(1024)S(1)}, f32[8192]{0:T(1024)}, u32[]{:S(2)}) copy-start(f32[8192]{0:T(1024)} %param.16) | copy-start | bytes 98308
  713.3 36.0 %copy-start.1 = (f32[128,64]{0,1:T(8,128)S(1)}, f32[128,64]{0,1:T(8,128)}, u32[]{:S(2)}) copy-start(f32[128,64]{0,1:T(8,128)} %custom-call.1) | copy-start | bytes 98308
  979.8 36.1 %copy-start.4 = (f32[4096]{0:T(1024)}, f32[4096]{0:T(1024)S(1)}, u32[]{:S(2)}) copy-start(f32[4096]{0:T(1024)S(1)} %add_subtract_fusion.3) | copy-start | bytes 49156
  979.9 36.0 %copy-start = (f32[128,64]{0,1:T(8,128)S(1)}, f32[128,64]{0,1:T(8,128)}, u32[]{:S(2)}) copy-start(f32[128,64]{0,1:T(8,128)} %custom-call.2) | copy-start | bytes 98308
Sparse Core Ops, SparseCore 0:
  23.1 33.5 all-gather.1
